TPU v7x, 256 devices: a whole 4x4x8 slice. The times are simulated.
256 devices in a mesh: gx: 16 (over x_lo, y, core), gy: 16 (over x_hi, z).
Axes of the slice: x: 4 (x_hi: 2, x_lo: 2; x = x_hi * 2 + x_lo), y: 4, z: 8, core: 2. Of those that a mesh axis runs over, the one named last changes fastest.
Arguments:
- velocity: float32 [3, 256, 128, 128], P(None, 'gx', 'gy'), may hold values from -24 to 24
- viscosity: float32 [256, 128, 128], P('gx', 'gy'), may hold values from 25 to 400
Outputs:
- half_step: float32 [3, 256, 128, 128], P(None, 'gx', 'gy')
- advanced: float32 [3, 256, 128, 128], P(None, 'gx', 'gy')
All inputs are finite; a program needn't handle non-finite values.
Results may differ from a plain program's by a relative error of at most 0.0003.
Values sent between devices are 32-bit elements; how exact they have to be, the bound alone decides.
A program may use at most 64 MiB of HBM per device.

v0:
```python
import jax
import jax.numpy as jnp
from jax import lax
from jax.experimental import pallas as pl
from jax.experimental.pallas import tpu as pltpu
from jax.sharding import PartitionSpec as P

MESH = pl.DeviceIdType.MESH
F32 = jnp.float32


class Network:
    def __init__(self):
        self.edge = {}
        self.ground = {}

    def join(self, a, b, w):
        k = (a, b) if a < b else (b, a)
        self.edge[k] = self.edge[k] + w if k in self.edge else w

    def add_ground(self, a, w):
        self.ground[a] = self.ground[a] + w if a in self.ground else w

    def eliminate(self, k):
        near = {}
        for a, b in list(self.edge):
            if k in (a, b):
                near[b if a == k else a] = self.edge.pop((a, b))
        ground = self.ground.pop(k)
        total = ground
        for w in near.values():
            total = total + w
        inverse = 1.0 / total
        ratio = {a: w * inverse for a, w in near.items()}
        names = sorted(near)
        for i, a in enumerate(names):
            self.add_ground(a, ratio[a] * ground)
            for b in names[i + 1 :]:
                self.join(a, b, ratio[a] * near[b])
        return k, inverse, ratio


def forward(step, source):
    k, inverse, ratio = step
    here = source.pop(k)
    for a, r in ratio.items():
        part = [r * h for h in here]
        source[a] = [s + t for s, t in zip(source[a], part)] if a in source else part
    return [h * inverse for h in here]


def summed(values):
    values = list(values)
    while len(values) > 1:
        values = [
            values[i] + values[i + 1] if i + 1 < len(values) else values[i]
            for i in range(0, len(values), 2)
        ]
    return values[0]


def responses(steps, own, terminals):
    base, unit = {}, {}
    for (k, inverse, ratio), y in reversed(list(zip(steps, own))):
        inner = [(a, r) for a, r in ratio.items() if a not in terminals]
        if y is not None:
            base[k] = [
                summed([y[c]] + [r * base[a][c] for a, r in inner]) for c in range(len(y))
            ]
        unit[k] = {}
        for t in terminals:
            terms = [r * unit[a][t] for a, r in inner if t in unit[a]]
            if t in ratio:
                terms.append(ratio[t])
            if terms:
                unit[k][t] = summed(terms)
    return base, unit


def kernel(
    vel, visc, half, adv,
    xmsg, xin, xret, xback, cmsg, cin, ymsg, yin, yret, yback, send, recv,
):
    gx, gy = lax.axis_index("gx"), lax.axis_index("gy")
    barrier = pltpu.get_barrier_semaphore()
    for axis, me in (("gy", gy), ("gx", gx)):
        for k in range(1, 16):
            pl.semaphore_signal(
                barrier, inc=1, device_id={axis: lax.rem(me + k, 16)}, device_id_type=MESH
            )

    lane_low = lax.broadcasted_iota(jnp.int32, (8, 128), 1) < 64
    row = lax.broadcasted_iota(jnp.int32, (8, 128), 0)

    def turn(x):
        return pltpu.roll(x, 64, 1)

    def pair(q1, q2):
        return jnp.where(lane_low, q1, turn(q2)), jnp.where(lane_low, turn(q1), q2)

    def exchange(axis, me, index, source, target, rows):
        for k in (8, 7, 9, 6, 10, 5, 11, 4, 12, 3, 13, 2, 14, 1, 15):
            peer = lax.rem(me + k, 16)
            pltpu.make_async_remote_copy(
                src_ref=source.at[pl.ds(pl.multiple_of(peer * rows, rows), rows)],
                dst_ref=target.at[pl.ds(pl.multiple_of(me * rows, rows), rows)],
                send_sem=send.at[index],
                recv_sem=recv.at[index],
                device_id={axis: peer},
                device_id_type=MESH,
            ).start()
        mine = pl.ds(pl.multiple_of(me * rows, rows), rows)
        target[mine, :] = source[mine, :]

    def arrived(index, target, rows):
        some = target.at[pl.ds(0, 15 * rows)]
        pltpu.make_async_copy(some, some, recv.at[index]).wait()

    def departed(index, source, rows):
        some = source.at[pl.ds(0, 15 * rows)]
        pltpu.make_async_copy(some, some, send.at[index]).wait()

    nu = [visc[pl.ds(8 * i, 8), :] for i in range(16)]
    net = Network()
    for i in range(16):
        net.add_ground(i, 1.0)
        if i < 15:
            net.join(i, i + 1, (nu[i] + nu[i + 1]) * 0.5)
        if i < 14:
            net.join(i, i + 2, (nu[i] + nu[i + 2]) * 0.125)
    source = {i: [vel[pl.ds(128 * c + 8 * i, 8), :] for c in range(3)] for i in range(16)}
    steps, own = [], []
    for k in (2, 13, 3, 12, 4, 11, 5, 10, 6, 9, 7, 8):
        step = net.eliminate(k)
        steps.append(step)
        own.append(forward(step, source))
    ends = (0, 1, 14, 15)
    out = [net.edge[e] for e in ((0, 1), (0, 14), (0, 15), (1, 14), (1, 15), (14, 15))]
    out += [net.ground[a] for a in ends] + [nu[a] for a in ends]
    out += [source[a][c] for a in ends for c in range(3)]
    for j in range(13):
        for side, value in enumerate(pair(out[2 * j], out[2 * j + 1])):
            xmsg[pl.ds(16 * side + j, 8, stride=32), :] = value
    for side in range(2):
        for j in range(13, 16):
            xmsg[pl.ds(16 * side + j, 8, stride=32), :] = jnp.zeros((8, 128), F32)

    eta = [visc[pl.ds(j, 16, stride=8), :] for j in range(8)]
    net = Network()
    for j in range(8):
        net.add_ground(j, 1.0)
        if j < 7:
            net.join(j, j + 1, eta[j] + eta[j + 1])
    net.add_ground(0, eta[0] * (gy == 0).astype(F32))
    net.add_ground(7, eta[7] * (gy == 15).astype(F32))
    ysteps = [net.eliminate(k) for k in (1, 6, 2, 5, 3, 4)]
    for j, value in enumerate((net.edge[(0, 7)], net.ground[0], net.ground[7], eta[0], eta[7])):
        cmsg[pl.ds(j, 16, stride=8), :] = value
    for j in range(5, 8):
        cmsg[pl.ds(j, 16, stride=8), :] = jnp.zeros((16, 128), F32)
        ymsg[pl.ds(j + (j == 5), 16, stride=8), :] = jnp.zeros((16, 128), F32)
        yret[pl.ds(j + (j == 5), 16, stride=8), :] = jnp.zeros((16, 128), F32)
    for j in range(6, 8):
        for side in range(2):
            xret[pl.ds(64 * side + j, 8, stride=8), :] = jnp.zeros((8, 128), F32)

    pl.semaphore_wait(barrier, 30)
    exchange("gx", gx, 0, xmsg, xin, 16)
    exchange("gy", gy, 1, cmsg, cin, 8)

    xbase, xunit = responses(steps, own, ends)
    unused, yunit = responses(ysteps, [None] * 6, (0, 7))

    arrived(0, xin, 16)
    got = []
    for j in range(13):
        got += pair(xin[pl.ds(j, 8, stride=16), :], xin[pl.ds(128 + j, 8, stride=16), :])
    ring = Network()
    names = ("a", "b", "c", "d")
    for e, (i, j) in enumerate(((0, 1), (0, 2), (0, 3), (1, 2), (1, 3), (2, 3))):
        ring.join(names[i], names[j], got[e])
    for i in range(4):
        ring.add_ground(names[i], got[6 + i])
    rhs = {names[i]: got[14 + 3 * i : 17 + 3 * i] for i in range(4)}
    nu0, nu1, nu14, nu15 = got[10:14]

    def after(x, h, turned=None):
        turned = turn(x) if turned is None else turned
        return turned if h == 8 else pltpu.roll(jnp.where(row >= h, x, turned), 8 - h, 0)

    def before(x, h, turned=None):
        turned = turn(x) if turned is None else turned
        return turned if h == 8 else pltpu.roll(jnp.where(row < 8 - h, x, turned), h, 0)

    last14, last15 = before(nu14, 1), before(nu15, 1)
    ring.join("a", "q", (last15 + nu0) * 0.5)
    ring.join("a", "p", (last14 + nu0) * 0.125)
    ring.join("b", "q", (last15 + nu1) * 0.125)
    rsteps = [ring.eliminate("a")]
    rown = [forward(rsteps[0], rhs)]
    rsteps.append(ring.eliminate("b"))
    rown.append(forward(rsteps[1], rhs))
    behind = [[ring.edge[("c", "p")], ring.edge[("c", "q")]], [ring.edge[("d", "p")], ring.edge[("d", "q")]]]
    onward = [[after(behind[j][i], 1) for j in range(2)] for i in range(2)]
    ground = [ring.ground["c"] + after(ring.ground["p"], 1), ring.ground["d"] + after(ring.ground["q"], 1)]
    inner = ring.edge[("c", "d")] + after(ring.edge[("p", "q")], 1)
    field = [
        [rhs[n][c] + after(rhs[m][c], 1) for c in range(3)] for n, m in (("c", "p"), ("d", "q"))
    ]

    def block_inverse(rest, link):
        scale = 1.0 / (rest[0] * rest[1] + link * (rest[0] + rest[1]))
        cross = link * scale
        return [[rest[1] * scale + cross, cross], [cross, rest[0] * scale + cross]]

    def times(m, v):
        return [[m[i][0] * v[0][j] + m[i][1] * v[1][j] for j in range(len(v[0]))] for i in range(2)]

    for h in (1, 2, 4):
        rest = [
            ground[i] + ((behind[i][0] + behind[i][1]) + (onward[i][0] + onward[i][1]))
            for i in range(2)
        ]
        inv = block_inverse(rest, inner)
        solved = times(inv, [[ground[i]] + field[i] + behind[i] + onward[i] for i in range(2)])
        turned = [[turn(x) for x in line] for line in solved]
        up = [[after(x, h, t) for x, t in zip(l, tl)] for l, tl in zip(solved, turned)]
        down = [[before(x, h, t) for x, t in zip(l, tl)] for l, tl in zip(solved, turned)]
        from_up, from_down = times(onward, up), times(behind, down)
        ground = [ground[i] + from_up[i][0] + from_down[i][0] for i in range(2)]
        field = [
            [field[i][c] + from_up[i][1 + c] + from_down[i][1 + c] for c in range(3)]
            for i in range(2)
        ]
        inner = inner + from_up[0][5] + from_down[0][7]
        onward = [from_up[i][6:8] for i in range(2)]
        behind = [from_down[i][4:6] for i in range(2)]
    across = [[behind[i][j] + onward[i][j] for j in range(2)] for i in range(2)]
    rest = [ground[i] + (across[i][0] + across[i][1]) for i in range(2)]
    inv = block_inverse(rest, inner)
    solved = times(inv, [[ground[i]] + field[i] + [across[i][1]] for i in range(2)])
    other = times(across, [[turn(x) for x in line] for line in solved])
    ground = [ground[i] + other[i][0] for i in range(2)]
    field = [[field[i][c] + other[i][1 + c] for c in range(3)] for i in range(2)]
    inner = inner + other[0][4]
    value_c, value_d = times(block_inverse(ground, inner), field)
    value = {"c": value_c, "d": value_d}
    value["p"] = [before(x, 1) for x in value_c]
    value["q"] = [before(x, 1) for x in value_d]
    for (k, unused, ratio), y in zip(rsteps[::-1], rown[::-1]):
        value[k] = [summed([y[c]] + [r * value[a][c] for a, r in ratio.items()]) for c in range(3)]
    out = [value[n][c] for n in names for c in range(3)]
    for j in range(6):
        for side, line in enumerate(pair(out[2 * j], out[2 * j + 1])):
            xret[pl.ds(64 * side + j, 8, stride=8), :] = line
    exchange("gx", gx, 2, xret, xback, 8)

    arrived(1, cin, 8)
    link, ground_a, ground_b, eta0, eta7 = [cin[pl.ds(j, 16, stride=8), :] for j in range(5)]
    segment = lax.broadcasted_iota(jnp.int32, (16, 128), 0)

    def lower(x, h):
        return pltpu.roll(x, h, 0)

    def upper(x, h):
        return pltpu.roll(x, 16 - h, 0)

    gate = jnp.where(segment == 0, 0.0, lower(eta7, 1) + eta0)
    inverse_a = 1.0 / (ground_a + link + gate)
    to_b, to_q = link * inverse_a, gate * inverse_a
    low = to_q * link
    high = jnp.where(segment == 15, 0.0, upper(low, 1))
    to_b_up = jnp.where(segment == 15, 0.0, upper(to_q, 1))
    ground = ground_b + to_b * ground_a + to_b_up * upper(ground_a, 1)
    sweeps = []
    for h in (1, 2, 4, 8):
        inverse = 1.0 / (ground + low + high)
        weight_low, weight_high = low * lower(inverse, h), high * upper(inverse, h)
        sweeps.append((h, weight_low, weight_high))
        ground = ground + weight_low * lower(ground, h) + weight_high * upper(ground, h)
        low, high = weight_low * lower(low, h), weight_high * upper(high, h)
    inverse_b = 1.0 / ground

    arrived(2, xback, 8)
    got = []
    for j in range(6):
        got += pair(xback[pl.ds(j, 8, stride=16), :], xback[pl.ds(8 + j, 8, stride=16), :])
    value = {a: got[3 * i : 3 * i + 3] for i, a in enumerate(ends)}
    for i in range(16):
        for c in range(3):
            if i in ends:
                x = value[i][c]
            else:
                x = summed([xbase[i][c]] + [w * value[a][c] for a, w in xunit[i].items()])
            half[pl.ds(128 * c + 8 * i, 8), :] = x

    lines = [[half[pl.ds(128 * c + j, 16, stride=8), :] for c in range(3)] for j in range(8)]
    for i, end in enumerate((0, 7)):
        for c in range(3):
            ymsg[pl.ds(3 * i + c, 16, stride=8), :] = summed(
                [lines[end][c]] + [yunit[k][end] * lines[k][c] for k in range(1, 7) if end in yunit[k]]
            )
    exchange("gy", gy, 3, ymsg, yin, 8)
    source = {j: list(lines[j]) for j in range(8)}
    yown = [forward(step, source) for step in ysteps]
    ybase, unused = responses(ysteps, yown, (0, 7))

    arrived(3, yin, 8)
    ends_a = [yin[pl.ds(c, 16, stride=8), :] for c in range(3)]
    ends_b = [yin[pl.ds(3 + c, 16, stride=8), :] for c in range(3)]
    for c in range(3):
        f = ends_b[c] + to_b * ends_a[c] + to_b_up * upper(ends_a[c], 1)
        for h, weight_low, weight_high in sweeps:
            f = f + weight_low * lower(f, h) + weight_high * upper(f, h)
        f = f * inverse_b
        yret[pl.ds(3 + c, 16, stride=8), :] = f
        yret[pl.ds(c, 16, stride=8), :] = inverse_a * ends_a[c] + to_b * f + to_q * lower(f, 1)
    exchange("gy", gy, 4, yret, yback, 8)

    arrived(4, yback, 8)
    first = [yback[pl.ds(c, 16, stride=8), :] for c in range(3)]
    final = [yback[pl.ds(3 + c, 16, stride=8), :] for c in range(3)]
    for c in range(3):
        for j in range(8):
            if j == 0:
                x = first[c]
            elif j == 7:
                x = final[c]
            else:
                x = ybase[j][c] + (yunit[j][0] * first[c] + yunit[j][7] * final[c])
            adv[pl.ds(128 * c + j, 16, stride=8), :] = x

    departed(0, xmsg, 16)
    departed(1, cmsg, 8)
    departed(2, xret, 8)
    departed(3, ymsg, 8)
    departed(4, yret, 8)


def on_device(velocity, viscosity):
    vmem = pl.BlockSpec(memory_space=pltpu.VMEM)
    small, large = pltpu.VMEM((128, 128), F32), pltpu.VMEM((256, 128), F32)
    half, adv = pl.pallas_call(
        kernel,
        name="adi",
        out_shape=[jax.ShapeDtypeStruct((384, 128), F32)] * 2,
        in_specs=[vmem, vmem],
        out_specs=[vmem, vmem],
        scratch_shapes=[large, large] + [small] * 8
        + [pltpu.SemaphoreType.DMA((5,)), pltpu.SemaphoreType.DMA((5,))],
        compiler_params=pltpu.CompilerParams(
            collective_id=0, has_side_effects=True, vmem_limit_bytes=32 * 1024 * 1024
        ),
    )(velocity.reshape(384, 128), viscosity.reshape(128, 128))
    return half.reshape(velocity.shape), adv.reshape(velocity.shape)


def solution(mesh):
    return jax.shard_map(
        on_device,
        mesh=mesh,
        in_specs=(P(None, "gx", "gy", None), P("gx", "gy", None)),
        out_specs=(P(None, "gx", "gy", None), P(None, "gx", "gy", None)),
        check_vma=False,
    )
```

profile of v0, /device:TPU:1, one launch (start us, length us, event | category | flops | bytes accessed | tf_op | source)
XLA Modules:
  0.0 35.4 jit_solution(3216472120076595280)
XLA Ops:
  0.6 0.0 copy-start
  0.6 0.9 %copy-done = f32[3,16,8,128]{3,2,1,0:T(8,128)S(1)} copy-done((f32[3,16,8,128]{3,2,1,0:T(8,128)S(1)}, f32[3,16,8,128]{3,2,1,0:T(8,128)}, u32[]{:S(2)}) %copy-start) | copy-done | bytes 196632
  1.6 0.0 copy-start.1
  1.6 0.8 %copy-done.1 = f32[16,8,128]{2,1,0:T(8,128)S(1)} copy-done((f32[16,8,128]{2,1,0:T(8,128)S(1)}, f32[16,8,128]{2,1,0:T(8,128)}, u32[]{:S(2)}) %copy-start.1) | copy-done | bytes 65560
  2.4 31.6 %adi.1 = (f32[384,128]{1,0:T(8,128)S(1)}, f32[384,128]{1,0:T(8,128)S(1)}) custom-call(f32[384,128]{1,0:T(8,128)S(1)} %bitcast.6, f32[128,128]{1,0:T(8,128)S(1)} %bitcast.7), custom_call_target="tpu_custom_call" | custom-call | tf_op jit(solution)/shard_map/adi/pallas_call | solution.py:343
  34.0 0.7 %copy.6 = f32[3,16,8,128]{3,2,1,0:T(8,128)} copy(f32[3,16,8,128]{3,2,1,0:T(8,128)S(1)} %bitcast.5) | data formatting | bytes 393216
  34.7 0.7 %copy.7 = f32[3,16,8,128]{3,2,1,0:T(8,128)} copy(f32[3,16,8,128]{3,2,1,0:T(8,128)S(1)} %bitcast.4) | data formatting | bytes 393216
Async XLA Ops:
  0.6 0.9 %copy-start = (f32[3,16,8,128]{3,2,1,0:T(8,128)S(1)}, f32[3,16,8,128]{3,2,1,0:T(8,128)}, u32[]{:S(2)}) copy-start(f32[3,16,8,128]{3,2,1,0:T(8,128)} %param.2) | copy-start | bytes 589828
  1.6 0.8 %copy-start.1 = (f32[16,8,128]{2,1,0:T(8,128)S(1)}, f32[16,8,128]{2,1,0:T(8,128)}, u32[]{:S(2)}) copy-start(f32[16,8,128]{2,1,0:T(8,128)} %param.3) | copy-start | bytes 196612
where the time goes:
time: 35.9 us; the launch traced here: 35.4 us
  Pallas kernels  31.6 us (88%)
  local copies, waits for them, and re-layouts  3.11 us (9%)
  between operations  0.65 us (2%)
    pallas_call x1, Pallas kernels, on_device(): pl.pallas_call(kernel, name='adi', out_shape=[jax.ShapeDtypeStruct((384,...  31.6 us
    unnamed x6, local copies, waits for them, and re-layouts  3.11 us

commit v1 on v0

--- a/solution.py
+++ b/solution.py
@@ -78,16 +78,28 @@
 
 
 def kernel(
-    vel, visc, half, adv,
-    xmsg, xin, xret, xback, cmsg, cin, ymsg, yin, yret, yback, send, recv,
+    vel_hbm, visc_hbm, half, adv,
+    vel, visc, load, xmsg, xin, xret, xback, cmsg, cin, ymsg, yin, yret, yback, send, recv, near, far,
 ):
     gx, gy = lax.axis_index("gx"), lax.axis_index("gy")
     barrier = pltpu.get_barrier_semaphore()
-    for axis, me in (("gy", gy), ("gx", gx)):
-        for k in range(1, 16):
-            pl.semaphore_signal(
-                barrier, inc=1, device_id={axis: lax.rem(me + k, 16)}, device_id_type=MESH
-            )
+    def place(side, move):
+        return lax.rem(gy // 8 + side, 2) * 8 + lax.rem(gy + 8 + move, 8)
+
+    def tell(semaphore, axis, peer):
+        pl.semaphore_signal(semaphore, inc=1, device_id={axis: peer}, device_id_type=MESH)
+
+    for peer in (place(0, 1), place(0, -1), place(1, 0), place(1, 1), place(1, -1)):
+        tell(barrier, "gy", peer)
+    for k in range(1, 16):
+        tell(barrier, "gx", lax.rem(gx + k, 16))
+
+    loads = [
+        pltpu.make_async_copy(visc_hbm, visc, load.at[0]),
+        pltpu.make_async_copy(vel_hbm, vel, load.at[1]),
+    ]
+    for copy in loads:
+        copy.start()
 
     lane_low = lax.broadcasted_iota(jnp.int32, (8, 128), 1) < 64
     row = lax.broadcasted_iota(jnp.int32, (8, 128), 0)
@@ -119,6 +131,9 @@
     def departed(index, source, rows):
         some = source.at[pl.ds(0, 15 * rows)]
         pltpu.make_async_copy(some, some, send.at[index]).wait()
+
+    for copy in loads:
+        copy.wait()
 
     nu = [visc[pl.ds(8 * i, 8), :] for i in range(16)]
     net = Network()
@@ -164,12 +179,17 @@
         for side in range(2):
             xret[pl.ds(64 * side + j, 8, stride=8), :] = jnp.zeros((8, 128), F32)
 
-    pl.semaphore_wait(barrier, 30)
+    pl.semaphore_wait(barrier, 20)
     exchange("gx", gx, 0, xmsg, xin, 16)
-    exchange("gy", gy, 1, cmsg, cin, 8)
+    tell(near, "gy", place(0, 1))
+    tell(near, "gy", place(0, -1))
 
     xbase, xunit = responses(steps, own, ends)
     unused, yunit = responses(ysteps, [None] * 6, (0, 7))
+
+    pl.semaphore_wait(near, 2)
+    tell(far, "gy", place(0, 2))
+    tell(far, "gy", place(0, -2))
 
     arrived(0, xin, 16)
     got = []
@@ -254,6 +274,32 @@
         for side, line in enumerate(pair(out[2 * j], out[2 * j + 1])):
             xret[pl.ds(64 * side + j, 8, stride=8), :] = line
     exchange("gx", gx, 2, xret, xback, 8)
+    pl.semaphore_wait(far, 2)
+    exchange("gy", gy, 1, cmsg, cin, 8)
+
+    arrived(2, xback, 8)
+    got = []
+    for j in range(6):
+        got += pair(xback[pl.ds(j, 8, stride=16), :], xback[pl.ds(8 + j, 8, stride=16), :])
+    value = {a: got[3 * i : 3 * i + 3] for i, a in enumerate(ends)}
+    for i in range(16):
+        for c in range(3):
+            if i in ends:
+                x = value[i][c]
+            else:
+                x = summed([xbase[i][c]] + [w * value[a][c] for a, w in xunit[i].items()])
+            half[pl.ds(128 * c + 8 * i, 8), :] = x
+
+    lines = [[half[pl.ds(128 * c + j, 16, stride=8), :] for c in range(3)] for j in range(8)]
+    for i, end in enumerate((0, 7)):
+        for c in range(3):
+            ymsg[pl.ds(3 * i + c, 16, stride=8), :] = summed(
+                [lines[end][c]] + [yunit[k][end] * lines[k][c] for k in range(1, 7) if end in yunit[k]]
+            )
+    exchange("gy", gy, 3, ymsg, yin, 8)
+    source = {j: list(lines[j]) for j in range(8)}
+    yown = [forward(step, source) for step in ysteps]
+    ybase, unused = responses(ysteps, yown, (0, 7))
 
     arrived(1, cin, 8)
     link, ground_a, ground_b, eta0, eta7 = [cin[pl.ds(j, 16, stride=8), :] for j in range(5)]
@@ -281,30 +327,6 @@
         low, high = weight_low * lower(low, h), weight_high * upper(high, h)
     inverse_b = 1.0 / ground
 
-    arrived(2, xback, 8)
-    got = []
-    for j in range(6):
-        got += pair(xback[pl.ds(j, 8, stride=16), :], xback[pl.ds(8 + j, 8, stride=16), :])
-    value = {a: got[3 * i : 3 * i + 3] for i, a in enumerate(ends)}
-    for i in range(16):
-        for c in range(3):
-            if i in ends:
-                x = value[i][c]
-            else:
-                x = summed([xbase[i][c]] + [w * value[a][c] for a, w in xunit[i].items()])
-            half[pl.ds(128 * c + 8 * i, 8), :] = x
-
-    lines = [[half[pl.ds(128 * c + j, 16, stride=8), :] for c in range(3)] for j in range(8)]
-    for i, end in enumerate((0, 7)):
-        for c in range(3):
-            ymsg[pl.ds(3 * i + c, 16, stride=8), :] = summed(
-                [lines[end][c]] + [yunit[k][end] * lines[k][c] for k in range(1, 7) if end in yunit[k]]
-            )
-    exchange("gy", gy, 3, ymsg, yin, 8)
-    source = {j: list(lines[j]) for j in range(8)}
-    yown = [forward(step, source) for step in ysteps]
-    ybase, unused = responses(ysteps, yown, (0, 7))
-
     arrived(3, yin, 8)
     ends_a = [yin[pl.ds(c, 16, stride=8), :] for c in range(3)]
     ends_b = [yin[pl.ds(3 + c, 16, stride=8), :] for c in range(3)]
@@ -337,21 +359,46 @@
     departed(4, yret, 8)
 
 
+def store(half, adv, half_hbm, adv_hbm, done):
+    copies = [
+        pltpu.make_async_copy(half, half_hbm, done.at[0]),
+        pltpu.make_async_copy(adv, adv_hbm, done.at[1]),
+    ]
+    for copy in copies:
+        copy.start()
+    for copy in copies:
+        copy.wait()
+
+
 def on_device(velocity, viscosity):
-    vmem = pl.BlockSpec(memory_space=pltpu.VMEM)
+    vmem, hbm = pl.BlockSpec(memory_space=pltpu.VMEM), pl.BlockSpec(memory_space=pltpu.HBM)
     small, large = pltpu.VMEM((128, 128), F32), pltpu.VMEM((256, 128), F32)
+    held = [
+        pltpu.with_memory_space_constraint(x, pltpu.HBM)
+        for x in (velocity.reshape(384, 128), viscosity.reshape(128, 128))
+    ]
     half, adv = pl.pallas_call(
         kernel,
         name="adi",
         out_shape=[jax.ShapeDtypeStruct((384, 128), F32)] * 2,
-        in_specs=[vmem, vmem],
+        in_specs=[hbm, hbm],
         out_specs=[vmem, vmem],
-        scratch_shapes=[large, large] + [small] * 8
-        + [pltpu.SemaphoreType.DMA((5,)), pltpu.SemaphoreType.DMA((5,))],
+        scratch_shapes=[pltpu.VMEM((384, 128), F32), small, pltpu.SemaphoreType.DMA((2,)), large, large] + [small] * 8
+        + [pltpu.SemaphoreType.DMA((5,)), pltpu.SemaphoreType.DMA((5,))]
+        + [pltpu.SemaphoreType.REGULAR] * 2,
         compiler_params=pltpu.CompilerParams(
             collective_id=0, has_side_effects=True, vmem_limit_bytes=32 * 1024 * 1024
         ),
-    )(velocity.reshape(384, 128), viscosity.reshape(128, 128))
+    )(*held)
+    half, adv = pl.pallas_call(
+        store,
+        name="store",
+        out_shape=[jax.ShapeDtypeStruct((384, 128), F32)] * 2,
+        in_specs=[vmem, vmem],
+        out_specs=[hbm, hbm],
+        scratch_shapes=[pltpu.SemaphoreType.DMA((2,))],
+        compiler_params=pltpu.CompilerParams(vmem_limit_bytes=1024 * 1024),
+    )(half, adv)
     return half.reshape(velocity.shape), adv.reshape(velocity.shape)
 
 

time: 35.9 us -> 31.7 us (0.88); the launches traced: 35.4 us -> 31.6 us
  local copies, waits for them, and re-layouts: 3.11 us -> 0 us
  Pallas kernels: 31.6 us -> 31 us
    unnamed x6 -> x0, local copies, waits for them, and re-layouts: 3.11 us -> none
    pallas_call x1, Pallas kernels: 31.6 us -> 30.2 us  [on_device(): pl.pallas_call(kernel, name='adi', out_shape=[jax.ShapeDtypeStruct((384,...]
    pallas_call x0 -> x1, Pallas kernels: none -> 0.76 us  [on_device(): pl.pallas_call(store, name='store', out_shape=[jax.ShapeDtypeStruct((384,...]
where the time goes in v1:
time: 31.7 us; the launch traced here: 31.6 us
  Pallas kernels  31 us (98%)
  between operations  0.64 us (2%)
    pallas_call x1, Pallas kernels, on_device(): pl.pallas_call(kernel, name='adi', out_shape=[jax.ShapeDtypeStruct((384,...  30.2 us
    pallas_call x1, Pallas kernels, on_device(): pl.pallas_call(store, name='store', out_shape=[jax.ShapeDtypeStruct((384,...  0.76 us

profile of v1, /device:TPU:1, one launch (start us, length us, event | category | flops | bytes accessed | tf_op | source)
XLA Modules:
  0.0 31.6 jit_solution(4885018036446338535)
XLA Ops:
  0.6 30.2 %adi.1 = (f32[384,128]{1,0:T(8,128)S(1)}, f32[384,128]{1,0:T(8,128)S(1)}) custom-call(f32[384,128]{1,0:T(8,128)} %bitcast.4, f32[128,128]{1,0:T(8,128)} %bitcast.5), custom_call_target="tpu_custom_call" | custom-call | tf_op jit(solution)/shard_map/adi/pallas_call | solution.py:380
  30.8 0.8 %store.1 = (f32[384,128]{1,0:T(8,128)}, f32[384,128]{1,0:T(8,128)}) custom-call(f32[384,128]{1,0:T(8,128)S(1)} %get-tuple-element.6.half, f32[384,128]{1,0:T(8,128)S(1)} %get-tuple-element.7.adv), custom_call_target="tpu_custom_call" | custom-call | tf_op jit(solution)/shard_map/store/pallas_call | solution.py:393

commit v2 on v1

v2 whole, which is shorter than its diff:
```python
import jax
import jax.numpy as jnp
from jax import lax
from jax.experimental import pallas as pl
from jax.experimental.pallas import tpu as pltpu
from jax.sharding import PartitionSpec as P

MESH = pl.DeviceIdType.MESH
F32 = jnp.float32


class Network:
    def __init__(self):
        self.edge = {}
        self.ground = {}

    def join(self, a, b, w):
        k = (a, b) if a < b else (b, a)
        self.edge[k] = self.edge[k] + w if k in self.edge else w

    def add_ground(self, a, w):
        self.ground[a] = self.ground[a] + w if a in self.ground else w

    def eliminate(self, k):
        near = {}
        for a, b in list(self.edge):
            if k in (a, b):
                near[b if a == k else a] = self.edge.pop((a, b))
        ground = self.ground.pop(k)
        total = ground
        for w in near.values():
            total = total + w
        inverse = 1.0 / total
        ratio = {a: w * inverse for a, w in near.items()}
        names = sorted(near)
        for i, a in enumerate(names):
            self.add_ground(a, ratio[a] * ground)
            for b in names[i + 1 :]:
                self.join(a, b, ratio[a] * near[b])
        return k, inverse, ratio


def forward(step, source):
    k, inverse, ratio = step
    here = source.pop(k)
    for a, r in ratio.items():
        part = [r * h for h in here]
        source[a] = [s + t for s, t in zip(source[a], part)] if a in source else part
    return [h * inverse for h in here]


def summed(values):
    values = list(values)
    while len(values) > 1:
        values = [
            values[i] + values[i + 1] if i + 1 < len(values) else values[i]
            for i in range(0, len(values), 2)
        ]
    return values[0]


def responses(steps, own, terminals):
    base, unit = {}, {}
    for (k, inverse, ratio), y in reversed(list(zip(steps, own))):
        inner = [(a, r) for a, r in ratio.items() if a not in terminals]
        if y is not None:
            base[k] = [
                summed([y[c]] + [r * base[a][c] for a, r in inner]) for c in range(len(y))
            ]
        unit[k] = {}
        for t in terminals:
            terms = [r * unit[a][t] for a, r in inner if t in unit[a]]
            if t in ratio:
                terms.append(ratio[t])
            if terms:
                unit[k][t] = summed(terms)
    return base, unit


def kernel(
    vel_hbm, visc_hbm, half, adv,
    vel, visc, load, xmsg, xin, xret, xback, cmsg, cin, ymsg, yin, yret, yback, send, recv, near, far, wide, go,
):
    gx, gy = lax.axis_index("gx"), lax.axis_index("gy")
    barrier = pltpu.get_barrier_semaphore()
    def place(side, move):
        return lax.rem(gy // 8 + side, 2) * 8 + lax.rem(gy + 8 + move, 8)

    def tell(semaphore, axis, peer):
        pl.semaphore_signal(semaphore, inc=1, device_id={axis: peer}, device_id_type=MESH)

    chip, core = gx // 2, lax.rem(gx, 2)

    around = (place(1, 1), place(1, -1), place(1, 0), place(0, 1), place(0, -1))

    @pl.when(core == 1)
    def announce():
        for peer in around:
            tell(barrier, "gy", peer)
        for k in (12, 4, 13, 11, 5, 3, 14, 10, 6, 2, 9, 7, 8, 1, 15):
            tell(barrier, "gx", lax.rem(gx + k, 16))

    @pl.when(core == 0)
    def report():
        tell(barrier, "gx", gx + 1)

    loads = [
        pltpu.make_async_copy(visc_hbm, visc, load.at[0]),
        pltpu.make_async_copy(vel_hbm, vel, load.at[1]),
    ]
    for copy in loads:
        copy.start()

    def push(index, source, start, target, to, rows, **place):
        pltpu.make_async_remote_copy(
            src_ref=source.at[pl.ds(pl.multiple_of(start, 8), rows)],
            dst_ref=target.at[pl.ds(pl.multiple_of(to, 8), rows)],
            send_sem=send.at[index],
            recv_sem=recv.at[index],
            device_id=place,
            device_id_type=MESH,
        ).start()

    def exchange(index, source, target):
        for k in (8, 7, 9, 6, 10, 5, 11, 4, 12, 3, 13, 2, 14, 1, 15):
            peer = lax.rem(gy + k, 16)
            push(index, source, peer * 8, target, gy * 8, 8, gy=peer)
        mine = pl.ds(pl.multiple_of(gy * 8, 8), 8)
        target[mine, :] = source[mine, :]

    def arrived(index, target, rows):
        some = target.at[pl.ds(0, rows)]
        pltpu.make_async_copy(some, some, recv.at[index]).wait()

    def departed(index, source, rows):
        some = source.at[pl.ds(0, rows)]
        pltpu.make_async_copy(some, some, send.at[index]).wait()

    for copy in loads:
        copy.wait()

    nu = [visc[pl.ds(8 * i, 8), :] for i in range(16)]
    net = Network()
    for i in range(16):
        net.add_ground(i, 1.0)
        if i < 15:
            net.join(i, i + 1, (nu[i] + nu[i + 1]) * 0.5)
        if i < 14:
            net.join(i, i + 2, (nu[i] + nu[i + 2]) * 0.125)
    source = {i: [vel[pl.ds(128 * c + 8 * i, 8), :] for c in range(3)] for i in range(16)}
    steps, own = [], []
    for k in (2, 13, 3, 12, 4, 11, 5, 10, 6, 9, 7, 8):
        step = net.eliminate(k)
        steps.append(step)
        own.append(forward(step, source))
    ends = (0, 1, 14, 15)
    out = [net.edge[e] for e in ((0, 1), (0, 14), (0, 15), (1, 14), (1, 15), (14, 15))]
    out += [net.ground[a] for a in ends] + [nu[a] for a in ends]
    out += [source[a][c] for a in ends for c in range(3)]
    for j, value in enumerate(out):
        xmsg[pl.ds(j, 8, stride=32), :] = value

    eta = [visc[pl.ds(j, 16, stride=8), :] for j in range(8)]
    net = Network()
    for j in range(8):
        net.add_ground(j, 1.0)
        if j < 7:
            net.join(j, j + 1, eta[j] + eta[j + 1])
    net.add_ground(0, eta[0] * (gy == 0).astype(F32))
    net.add_ground(7, eta[7] * (gy == 15).astype(F32))
    ysteps = [net.eliminate(k) for k in (1, 6, 2, 5, 3, 4)]
    for j, value in enumerate((net.edge[(0, 7)], net.ground[0], net.ground[7], eta[0], eta[7])):
        cmsg[pl.ds(j, 16, stride=8), :] = value
    for j in range(5, 8):
        cmsg[pl.ds(j, 16, stride=8), :] = jnp.zeros((16, 128), F32)
        ymsg[pl.ds(j + (j == 5), 16, stride=8), :] = jnp.zeros((16, 128), F32)
        yret[pl.ds(j + (j == 5), 16, stride=8), :] = jnp.zeros((16, 128), F32)

    pl.semaphore_wait(barrier, 8 + 5 * core)
    for k in (4, 3, 5, 2, 6, 1, 7):
        peer = lax.rem(chip + k, 8)
        push(0, xmsg, peer * 32, xin, gx * 32, 26, gx=peer * 2 + 1)

    @pl.when(core == 0)
    def lend():
        push(0, xmsg, chip * 32, xin, gx * 32, 26, gx=gx + 1)

    @pl.when(core == 1)
    def keep():
        for peer in around:
            tell(near, "gy", peer)
        xin[pl.ds(pl.multiple_of(gx * 32, 8), 26), :] = xmsg[
            pl.ds(pl.multiple_of(chip * 32, 8), 26), :
        ]

    xbase, xunit = responses(steps, own, ends)
    unused, yunit = responses(ysteps, [None] * 6, (0, 7))

    @pl.when(core == 1)
    def solve_ring():
        pl.semaphore_wait(near, 5)
        tell(far, "gy", place(0, 2))
        tell(far, "gy", place(0, -2))

        arrived(0, xin, 15 * 26)
        got = [xin[pl.ds(j, 16, stride=32), :] for j in range(26)]
        ring = Network()
        names = ("a", "b", "c", "d")
        for e, (i, j) in enumerate(((0, 1), (0, 2), (0, 3), (1, 2), (1, 3), (2, 3))):
            ring.join(names[i], names[j], got[e])
        for i in range(4):
            ring.add_ground(names[i], got[6 + i])
        rhs = {names[i]: got[14 + 3 * i : 17 + 3 * i] for i in range(4)}
        nu0, nu1, nu14, nu15 = got[10:14]

        def after(x, h):
            return pltpu.roll(x, 16 - h, 0)

        def before(x, h):
            return pltpu.roll(x, h, 0)

        last14, last15 = before(nu14, 1), before(nu15, 1)
        ring.join("a", "q", (last15 + nu0) * 0.5)
        ring.join("a", "p", (last14 + nu0) * 0.125)
        ring.join("b", "q", (last15 + nu1) * 0.125)
        rsteps = [ring.eliminate("a")]
        rown = [forward(rsteps[0], rhs)]
        rsteps.append(ring.eliminate("b"))
        rown.append(forward(rsteps[1], rhs))
        behind = [[ring.edge[("c", "p")], ring.edge[("c", "q")]], [ring.edge[("d", "p")], ring.edge[("d", "q")]]]
        onward = [[after(behind[j][i], 1) for j in range(2)] for i in range(2)]
        ground = [ring.ground["c"] + after(ring.ground["p"], 1), ring.ground["d"] + after(ring.ground["q"], 1)]
        inner = ring.edge[("c", "d")] + after(ring.edge[("p", "q")], 1)
        field = [
            [rhs[n][c] + after(rhs[m][c], 1) for c in range(3)] for n, m in (("c", "p"), ("d", "q"))
        ]

        def block_inverse(rest, link):
            scale = 1.0 / (rest[0] * rest[1] + link * (rest[0] + rest[1]))
            cross = link * scale
            return [[rest[1] * scale + cross, cross], [cross, rest[0] * scale + cross]]

        def times(m, v):
            return [[m[i][0] * v[0][j] + m[i][1] * v[1][j] for j in range(len(v[0]))] for i in range(2)]

        for h in (1, 2, 4):
            rest = [
                ground[i] + ((behind[i][0] + behind[i][1]) + (onward[i][0] + onward[i][1]))
                for i in range(2)
            ]
            inv = block_inverse(rest, inner)
            solved = times(inv, [[ground[i]] + field[i] + behind[i] + onward[i] for i in range(2)])
            up = [[after(x, h) for x in line] for line in solved]
            down = [[before(x, h) for x in line] for line in solved]
            from_up, from_down = times(onward, up), times(behind, down)
            ground = [ground[i] + from_up[i][0] + from_down[i][0] for i in range(2)]
            field = [
                [field[i][c] + from_up[i][1 + c] + from_down[i][1 + c] for c in range(3)]
                for i in range(2)
            ]
            inner = inner + from_up[0][5] + from_down[0][7]
            onward = [from_up[i][6:8] for i in range(2)]
            behind = [from_down[i][4:6] for i in range(2)]
        across = [[behind[i][j] + onward[i][j] for j in range(2)] for i in range(2)]
        rest = [ground[i] + (across[i][0] + across[i][1]) for i in range(2)]
        inv = block_inverse(rest, inner)
        solved = times(inv, [[ground[i]] + field[i] + [across[i][1]] for i in range(2)])
        other = times(across, [[after(x, 8) for x in line] for line in solved])
        ground = [ground[i] + other[i][0] for i in range(2)]
        field = [[field[i][c] + other[i][1 + c] for c in range(3)] for i in range(2)]
        inner = inner + other[0][4]
        value_c, value_d = times(block_inverse(ground, inner), field)
        value = {"c": value_c, "d": value_d}
        value["p"] = [before(x, 1) for x in value_c]
        value["q"] = [before(x, 1) for x in value_d]
        for (k, unused, ratio), y in zip(rsteps[::-1], rown[::-1]):
            value[k] = [summed([y[c]] + [r * value[a][c] for a, r in ratio.items()]) for c in range(3)]
        out = [value[n][c] for n in names for c in range(3)]
        for j, line in enumerate(out):
            xret[pl.ds(j, 16, stride=16), :] = line
        for k in (8, 7, 9, 5, 11, 4, 12, 3, 13, 6, 10, 2, 14, 1, 15):
            peer = lax.rem(gx + k, 16)
            push(2, xret, peer * 16, xback, chip * 16, 12, gx=peer)
        xback[pl.ds(pl.multiple_of(chip * 16, 8), 12), :] = xret[
            pl.ds(pl.multiple_of(gx * 16, 8), 12), :
        ]
        pl.semaphore_wait(far, 2)
        tell(wide, "gy", place(0, 1))
        tell(wide, "gy", place(0, -1))
        pl.semaphore_wait(wide, 2)
        tell(go, "gx", gx - 1)

    @pl.when(core == 0)
    def follow():
        pl.semaphore_wait(go, 1)

    exchange(1, cmsg, cin)

    @pl.when(core == 1)
    def seven():
        arrived(2, xback, 7 * 12)

    @pl.when(core == 0)
    def eight():
        arrived(2, xback, 8 * 12)

    got = [xback[pl.ds(j, 8, stride=16), :] for j in range(12)]
    value = {a: got[3 * i : 3 * i + 3] for i, a in enumerate(ends)}
    for i in range(16):
        for c in range(3):
            if i in ends:
                x = value[i][c]
            else:
                x = summed([xbase[i][c]] + [w * value[a][c] for a, w in xunit[i].items()])
            half[pl.ds(128 * c + 8 * i, 8), :] = x

    lines = [[half[pl.ds(128 * c + j, 16, stride=8), :] for c in range(3)] for j in range(8)]
    for i, end in enumerate((0, 7)):
        for c in range(3):
            ymsg[pl.ds(3 * i + c, 16, stride=8), :] = summed(
                [lines[end][c]] + [yunit[k][end] * lines[k][c] for k in range(1, 7) if end in yunit[k]]
            )
    exchange(3, ymsg, yin)
    source = {j: list(lines[j]) for j in range(8)}
    yown = [forward(step, source) for step in ysteps]
    ybase, unused = responses(ysteps, yown, (0, 7))

    arrived(1, cin, 15 * 8)
    link, ground_a, ground_b, eta0, eta7 = [cin[pl.ds(j, 16, stride=8), :] for j in range(5)]
    segment = lax.broadcasted_iota(jnp.int32, (16, 128), 0)

    def lower(x, h):
        return pltpu.roll(x, h, 0)

    def upper(x, h):
        return pltpu.roll(x, 16 - h, 0)

    gate = jnp.where(segment == 0, 0.0, lower(eta7, 1) + eta0)
    inverse_a = 1.0 / (ground_a + link + gate)
    to_b, to_q = link * inverse_a, gate * inverse_a
    low = to_q * link
    high = jnp.where(segment == 15, 0.0, upper(low, 1))
    to_b_up = jnp.where(segment == 15, 0.0, upper(to_q, 1))
    ground = ground_b + to_b * ground_a + to_b_up * upper(ground_a, 1)
    sweeps = []
    for h in (1, 2, 4, 8):
        inverse = 1.0 / (ground + low + high)
        weight_low, weight_high = low * lower(inverse, h), high * upper(inverse, h)
        sweeps.append((h, weight_low, weight_high))
        ground = ground + weight_low * lower(ground, h) + weight_high * upper(ground, h)
        low, high = weight_low * lower(low, h), weight_high * upper(high, h)
    inverse_b = 1.0 / ground

    arrived(3, yin, 15 * 8)
    ends_a = [yin[pl.ds(c, 16, stride=8), :] for c in range(3)]
    ends_b = [yin[pl.ds(3 + c, 16, stride=8), :] for c in range(3)]
    for c in range(3):
        f = ends_b[c] + to_b * ends_a[c] + to_b_up * upper(ends_a[c], 1)
        for h, weight_low, weight_high in sweeps:
            f = f + weight_low * lower(f, h) + weight_high * upper(f, h)
        f = f * inverse_b
        yret[pl.ds(3 + c, 16, stride=8), :] = f
        yret[pl.ds(c, 16, stride=8), :] = inverse_a * ends_a[c] + to_b * f + to_q * lower(f, 1)
    exchange(4, yret, yback)

    arrived(4, yback, 15 * 8)
    first = [yback[pl.ds(c, 16, stride=8), :] for c in range(3)]
    final = [yback[pl.ds(3 + c, 16, stride=8), :] for c in range(3)]
    for c in range(3):
        for j in range(8):
            if j == 0:
                x = first[c]
            elif j == 7:
                x = final[c]
            else:
                x = ybase[j][c] + (yunit[j][0] * first[c] + yunit[j][7] * final[c])
            adv[pl.ds(128 * c + j, 16, stride=8), :] = x

    departed(0, xmsg, 7 * 26)
    departed(1, cmsg, 15 * 8)
    departed(3, ymsg, 15 * 8)
    departed(4, yret, 15 * 8)

    @pl.when(core == 0)
    def lent():
        departed(0, xmsg, 26)

    @pl.when(core == 1)
    def returned():
        departed(2, xret, 15 * 12)


def store(half, adv, half_hbm, adv_hbm, done):
    copies = [
        pltpu.make_async_copy(half, half_hbm, done.at[0]),
        pltpu.make_async_copy(adv, adv_hbm, done.at[1]),
    ]
    for copy in copies:
        copy.start()
    for copy in copies:
        copy.wait()


def on_device(velocity, viscosity):
    vmem, hbm = pl.BlockSpec(memory_space=pltpu.VMEM), pl.BlockSpec(memory_space=pltpu.HBM)
    small, large = pltpu.VMEM((128, 128), F32), pltpu.VMEM((256, 128), F32)
    huge = pltpu.VMEM((512, 128), F32)
    held = [
        pltpu.with_memory_space_constraint(x, pltpu.HBM)
        for x in (velocity.reshape(384, 128), viscosity.reshape(128, 128))
    ]
    half, adv = pl.pallas_call(
        kernel,
        name="adi",
        out_shape=[jax.ShapeDtypeStruct((384, 128), F32)] * 2,
        in_specs=[hbm, hbm],
        out_specs=[vmem, vmem],
        scratch_shapes=[pltpu.VMEM((384, 128), F32), small, pltpu.SemaphoreType.DMA((2,)), large, huge, large] + [small] * 7
        + [pltpu.SemaphoreType.DMA((5,)), pltpu.SemaphoreType.DMA((5,))]
        + [pltpu.SemaphoreType.REGULAR] * 4,
        compiler_params=pltpu.CompilerParams(
            collective_id=0, has_side_effects=True, vmem_limit_bytes=32 * 1024 * 1024
        ),
    )(*held)
    half, adv = pl.pallas_call(
        store,
        name="store",
        out_shape=[jax.ShapeDtypeStruct((384, 128), F32)] * 2,
        in_specs=[vmem, vmem],
        out_specs=[hbm, hbm],
        scratch_shapes=[pltpu.SemaphoreType.DMA((2,))],
        compiler_params=pltpu.CompilerParams(vmem_limit_bytes=1024 * 1024),
    )(half, adv)
    return half.reshape(velocity.shape), adv.reshape(velocity.shape)


def solution(mesh):
    return jax.shard_map(
        on_device,
        mesh=mesh,
        in_specs=(P(None, "gx", "gy", None), P("gx", "gy", None)),
        out_specs=(P(None, "gx", "gy", None), P(None, "gx", "gy", None)),
        check_vma=False,
    )
```

time: 31.7 us -> 29.4 us (0.927)
  Pallas kernels: 31 us -> 28.6 us
    pallas_call x1, Pallas kernels: 30.2 us -> 27.9 us  [on_device(): pl.pallas_call(kernel, name='adi', out_shape=[jax.ShapeDtypeStruct((384,...]
where the time goes in v2:
time: 29.4 us; the launch traced here: 29.3 us
  Pallas kernels  28.6 us (97%)
  between operations  0.64 us (2%)
    pallas_call x1, Pallas kernels, on_device(): pl.pallas_call(kernel, name='adi', out_shape=[jax.ShapeDtypeStruct((384,...  27.9 us
    pallas_call x1, Pallas kernels, on_device(): pl.pallas_call(store, name='store', out_shape=[jax.ShapeDtypeStruct((384,...  0.76 us

profile of v2, /device:TPU:1, one launch (start us, length us, event | category | flops | bytes accessed | tf_op | source)
XLA Modules:
  0.0 29.3 jit_solution(7047659635613699091)
XLA Ops:
  0.6 27.9 %adi.1 = (f32[384,128]{1,0:T(8,128)S(1)}, f32[384,128]{1,0:T(8,128)S(1)}) custom-call(f32[384,128]{1,0:T(8,128)} %bitcast.4, f32[128,128]{1,0:T(8,128)} %bitcast.5), custom_call_target="tpu_custom_call" | custom-call | tf_op jit(solution)/shard_map/adi/pallas_call | solution.py:412
  28.5 0.8 %store.1 = (f32[384,128]{1,0:T(8,128)}, f32[384,128]{1,0:T(8,128)}) custom-call(f32[384,128]{1,0:T(8,128)S(1)} %get-tuple-element.6.half, f32[384,128]{1,0:T(8,128)S(1)} %get-tuple-element.7.adv), custom_call_target="tpu_custom_call" | custom-call | tf_op jit(solution)/shard_map/store/pallas_call | solution.py:425

commit v3 on v2

--- a/solution.py
+++ b/solution.py
@@ -6,6 +6,8 @@
 from jax.sharding import PartitionSpec as P
 
 MESH = pl.DeviceIdType.MESH
+PLACES = (6, 7, 0, 1)
+SOLVERS = tuple(8 * side + p for side in range(2) for p in PLACES)
 F32 = jnp.float32
 
 
@@ -113,7 +115,7 @@
 
     def push(index, source, start, target, to, rows, **place):
         pltpu.make_async_remote_copy(
-            src_ref=source.at[pl.ds(pl.multiple_of(start, 8), rows)],
+            src_ref=source.at[pl.ds(start if isinstance(start, int) else pl.multiple_of(start, 8), rows)],
             dst_ref=target.at[pl.ds(pl.multiple_of(to, 8), rows)],
             send_sem=send.at[index],
             recv_sem=recv.at[index],
@@ -121,12 +123,42 @@
             device_id_type=MESH,
         ).start()
 
-    def exchange(index, source, target):
-        for k in (8, 7, 9, 6, 10, 5, 11, 4, 12, 3, 13, 2, 14, 1, 15):
-            peer = lax.rem(gy + k, 16)
-            push(index, source, peer * 8, target, gy * 8, 8, gy=peer)
-        mine = pl.ds(pl.multiple_of(gy * 8, 8), 8)
-        target[mine, :] = source[mine, :]
+    spot = lax.rem(gy, 8)
+    solves = (spot == PLACES[0]) | (spot == PLACES[1]) | (spot == PLACES[2]) | (spot == PLACES[3])
+    rank = (gy // 8) * 4 + sum(i * (spot == p).astype(jnp.int32) for i, p in enumerate(PLACES))
+
+    def stay(source, start, target, to, rows):
+        target[pl.ds(pl.multiple_of(to, 8), rows), :] = source[
+            pl.ds(pl.multiple_of(start, 8), rows), :
+        ]
+
+    def hand_in(index, source, target, rows):
+        for at in (0, 4, 3, 7, 1, 5, 2, 6):
+
+            @pl.when(gy != SOLVERS[at])
+            def lend_row(at=at):
+                push(index, source, 16 * at, target, gy * 16, rows, gy=SOLVERS[at])
+
+        @pl.when(solves)
+        def keep_row():
+            stay(source, rank * 16, target, gy * 16, rows)
+
+    def hand_back(index, source, target, rows):
+        for at in (0, 8, 1, 9, 2, 10, 3, 11, 7, 15, 6, 14, 5, 13, 4, 12):
+
+            @pl.when(gy != at)
+            def return_row(at=at):
+                push(index, source, 16 * at, target, rank * 16, rows, gy=at)
+
+        stay(source, gy * 16, target, rank * 16, rows)
+
+    def by_row(ref, name, rows, value=None):
+        if value is None:
+            return jnp.concatenate(
+                [ref[pl.ds(rows * r + name, 8, stride=16), :] for r in range(2)], axis=0
+            )
+        for r in range(2):
+            ref[pl.ds(rows * r + name, 8, stride=16), :] = value[8 * r : 8 * r + 8]
 
     def arrived(index, target, rows):
         some = target.at[pl.ds(0, rows)]
@@ -160,6 +192,23 @@
     for j, value in enumerate(out):
         xmsg[pl.ds(j, 8, stride=32), :] = value
 
+    pl.semaphore_wait(barrier, 8 + 5 * core)
+    for k in (4, 3, 5, 2, 6, 1, 7):
+        peer = lax.rem(chip + k, 8)
+        push(0, xmsg, peer * 32, xin, gx * 32, 26, gx=peer * 2 + 1)
+
+    @pl.when(core == 0)
+    def lend():
+        push(0, xmsg, chip * 32, xin, gx * 32, 26, gx=gx + 1)
+
+    @pl.when(core == 1)
+    def keep():
+        for peer in around:
+            tell(near, "gy", peer)
+        xin[pl.ds(pl.multiple_of(gx * 32, 8), 26), :] = xmsg[
+            pl.ds(pl.multiple_of(chip * 32, 8), 26), :
+        ]
+
     eta = [visc[pl.ds(j, 16, stride=8), :] for j in range(8)]
     net = Network()
     for j in range(8):
@@ -170,28 +219,7 @@
     net.add_ground(7, eta[7] * (gy == 15).astype(F32))
     ysteps = [net.eliminate(k) for k in (1, 6, 2, 5, 3, 4)]
     for j, value in enumerate((net.edge[(0, 7)], net.ground[0], net.ground[7], eta[0], eta[7])):
-        cmsg[pl.ds(j, 16, stride=8), :] = value
-    for j in range(5, 8):
-        cmsg[pl.ds(j, 16, stride=8), :] = jnp.zeros((16, 128), F32)
-        ymsg[pl.ds(j + (j == 5), 16, stride=8), :] = jnp.zeros((16, 128), F32)
-        yret[pl.ds(j + (j == 5), 16, stride=8), :] = jnp.zeros((16, 128), F32)
-
-    pl.semaphore_wait(barrier, 8 + 5 * core)
-    for k in (4, 3, 5, 2, 6, 1, 7):
-        peer = lax.rem(chip + k, 8)
-        push(0, xmsg, peer * 32, xin, gx * 32, 26, gx=peer * 2 + 1)
-
-    @pl.when(core == 0)
-    def lend():
-        push(0, xmsg, chip * 32, xin, gx * 32, 26, gx=gx + 1)
-
-    @pl.when(core == 1)
-    def keep():
-        for peer in around:
-            tell(near, "gy", peer)
-        xin[pl.ds(pl.multiple_of(gx * 32, 8), 26), :] = xmsg[
-            pl.ds(pl.multiple_of(chip * 32, 8), 26), :
-        ]
+        by_row(cmsg, j, 5, value)
 
     xbase, xunit = responses(steps, own, ends)
     unused, yunit = responses(ysteps, [None] * 6, (0, 7))
@@ -294,7 +322,7 @@
     def follow():
         pl.semaphore_wait(go, 1)
 
-    exchange(1, cmsg, cin)
+    hand_in(1, cmsg, cin, 10)
 
     @pl.when(core == 1)
     def seven():
@@ -317,16 +345,15 @@
     lines = [[half[pl.ds(128 * c + j, 16, stride=8), :] for c in range(3)] for j in range(8)]
     for i, end in enumerate((0, 7)):
         for c in range(3):
-            ymsg[pl.ds(3 * i + c, 16, stride=8), :] = summed(
+            value = summed(
                 [lines[end][c]] + [yunit[k][end] * lines[k][c] for k in range(1, 7) if end in yunit[k]]
             )
-    exchange(3, ymsg, yin)
+            by_row(ymsg, 3 * i + c, 6, value)
+    hand_in(3, ymsg, yin, 12)
     source = {j: list(lines[j]) for j in range(8)}
     yown = [forward(step, source) for step in ysteps]
     ybase, unused = responses(ysteps, yown, (0, 7))
 
-    arrived(1, cin, 15 * 8)
-    link, ground_a, ground_b, eta0, eta7 = [cin[pl.ds(j, 16, stride=8), :] for j in range(5)]
     segment = lax.broadcasted_iota(jnp.int32, (16, 128), 0)
 
     def lower(x, h):
@@ -335,37 +362,56 @@
     def upper(x, h):
         return pltpu.roll(x, 16 - h, 0)
 
-    gate = jnp.where(segment == 0, 0.0, lower(eta7, 1) + eta0)
-    inverse_a = 1.0 / (ground_a + link + gate)
-    to_b, to_q = link * inverse_a, gate * inverse_a
-    low = to_q * link
-    high = jnp.where(segment == 15, 0.0, upper(low, 1))
-    to_b_up = jnp.where(segment == 15, 0.0, upper(to_q, 1))
-    ground = ground_b + to_b * ground_a + to_b_up * upper(ground_a, 1)
-    sweeps = []
-    for h in (1, 2, 4, 8):
-        inverse = 1.0 / (ground + low + high)
-        weight_low, weight_high = low * lower(inverse, h), high * upper(inverse, h)
-        sweeps.append((h, weight_low, weight_high))
-        ground = ground + weight_low * lower(ground, h) + weight_high * upper(ground, h)
-        low, high = weight_low * lower(low, h), weight_high * upper(high, h)
-    inverse_b = 1.0 / ground
-
-    arrived(3, yin, 15 * 8)
-    ends_a = [yin[pl.ds(c, 16, stride=8), :] for c in range(3)]
-    ends_b = [yin[pl.ds(3 + c, 16, stride=8), :] for c in range(3)]
-    for c in range(3):
-        f = ends_b[c] + to_b * ends_a[c] + to_b_up * upper(ends_a[c], 1)
-        for h, weight_low, weight_high in sweeps:
-            f = f + weight_low * lower(f, h) + weight_high * upper(f, h)
-        f = f * inverse_b
-        yret[pl.ds(3 + c, 16, stride=8), :] = f
-        yret[pl.ds(c, 16, stride=8), :] = inverse_a * ends_a[c] + to_b * f + to_q * lower(f, 1)
-    exchange(4, yret, yback)
-
-    arrived(4, yback, 15 * 8)
-    first = [yback[pl.ds(c, 16, stride=8), :] for c in range(3)]
-    final = [yback[pl.ds(3 + c, 16, stride=8), :] for c in range(3)]
+    def factor(r):
+        link, ground_a, ground_b, eta0, eta7 = [
+            cin[pl.ds(5 * r + j, 16, stride=16), :] for j in range(5)
+        ]
+        gate = jnp.where(segment == 0, 0.0, lower(eta7, 1) + eta0)
+        inverse_a = 1.0 / (ground_a + link + gate)
+        to_b, to_q = link * inverse_a, gate * inverse_a
+        low = to_q * link
+        high = jnp.where(segment == 15, 0.0, upper(low, 1))
+        to_b_up = jnp.where(segment == 15, 0.0, upper(to_q, 1))
+        ground = ground_b + to_b * ground_a + to_b_up * upper(ground_a, 1)
+        sweeps = []
+        for h in (1, 2, 4, 8):
+            inverse = 1.0 / (ground + low + high)
+            weight_low, weight_high = low * lower(inverse, h), high * upper(inverse, h)
+            sweeps.append((h, weight_low, weight_high))
+            ground = ground + weight_low * lower(ground, h) + weight_high * upper(ground, h)
+            low, high = weight_low * lower(low, h), weight_high * upper(high, h)
+        return inverse_a, to_b, to_q, to_b_up, sweeps, 1.0 / ground
+
+    def solve_row(r, factors):
+        inverse_a, to_b, to_q, to_b_up, sweeps, inverse_b = factors
+        for c in range(3):
+            end_a = yin[pl.ds(6 * r + c, 16, stride=16), :]
+            f = yin[pl.ds(6 * r + 3 + c, 16, stride=16), :]
+            f = f + to_b * end_a + to_b_up * upper(end_a, 1)
+            for h, weight_low, weight_high in sweeps:
+                f = f + weight_low * lower(f, h) + weight_high * upper(f, h)
+            f = f * inverse_b
+            yret[pl.ds(6 * r + 3 + c, 16, stride=16), :] = f
+            yret[pl.ds(6 * r + c, 16, stride=16), :] = (
+                inverse_a * end_a + to_b * f + to_q * lower(f, 1)
+            )
+
+    @pl.when(solves)
+    def solve_rows():
+        arrived(1, cin, 15 * 10)
+        factors = [factor(r) for r in range(2)]
+        arrived(3, yin, 15 * 12)
+        for r in range(2):
+            solve_row(r, factors[r])
+        hand_back(4, yret, yback, 12)
+        arrived(4, yback, 7 * 12)
+
+    @pl.when(jnp.logical_not(solves))
+    def await_rows():
+        arrived(4, yback, 8 * 12)
+
+    first = [by_row(yback, c, 6) for c in range(3)]
+    final = [by_row(yback, 3 + c, 6) for c in range(3)]
     for c in range(3):
         for j in range(8):
             if j == 0:
@@ -377,9 +423,17 @@
             adv[pl.ds(128 * c + j, 16, stride=8), :] = x
 
     departed(0, xmsg, 7 * 26)
-    departed(1, cmsg, 15 * 8)
-    departed(3, ymsg, 15 * 8)
-    departed(4, yret, 15 * 8)
+    departed(1, cmsg, 7 * 10)
+    departed(3, ymsg, 7 * 12)
+
+    @pl.when(solves)
+    def answered():
+        departed(4, yret, 15 * 12)
+
+    @pl.when(jnp.logical_not(solves))
+    def asked():
+        departed(1, cmsg, 10)
+        departed(3, ymsg, 12)
 
     @pl.when(core == 0)
     def lent():
@@ -415,7 +469,7 @@
         out_shape=[jax.ShapeDtypeStruct((384, 128), F32)] * 2,
         in_specs=[hbm, hbm],
         out_specs=[vmem, vmem],
-        scratch_shapes=[pltpu.VMEM((384, 128), F32), small, pltpu.SemaphoreType.DMA((2,)), large, huge, large] + [small] * 7
+        scratch_shapes=[pltpu.VMEM((384, 128), F32), small, pltpu.SemaphoreType.DMA((2,)), large, huge, large, small, small, large, small, large, large, small]
         + [pltpu.SemaphoreType.DMA((5,)), pltpu.SemaphoreType.DMA((5,))]
         + [pltpu.SemaphoreType.REGULAR] * 4,
         compiler_params=pltpu.CompilerParams(

time: 29.4 us -> 28.4 us (0.966)
  Pallas kernels: 28.6 us -> 27.5 us
    pallas_call x1, Pallas kernels: 27.9 us -> 26.7 us  [on_device(): pl.pallas_call(kernel, name='adi', out_shape=[jax.ShapeDtypeStruct((384,...]
where the time goes in v3:
time: 28.4 us; the launch traced here: 28.1 us
  Pallas kernels  27.5 us (97%)
  between operations  0.64 us (2%)
    pallas_call x1, Pallas kernels, on_device(): pl.pallas_call(kernel, name='adi', out_shape=[jax.ShapeDtypeStruct((384,...  26.7 us
    pallas_call x1, Pallas kernels, on_device(): pl.pallas_call(store, name='store', out_shape=[jax.ShapeDtypeStruct((384,...  0.76 us

profile of v3, /device:TPU:1, one launch (start us, length us, event | category | flops | bytes accessed | tf_op | source)
XLA Modules:
  0.0 28.1 jit_solution(2332721764846294938)
XLA Ops:
  0.6 26.7 %adi.1 = (f32[384,128]{1,0:T(8,128)S(1)}, f32[384,128]{1,0:T(8,128)S(1)}) custom-call(f32[384,128]{1,0:T(8,128)} %bitcast.4, f32[128,128]{1,0:T(8,128)} %bitcast.5), custom_call_target="tpu_custom_call" | custom-call | tf_op jit(solution)/shard_map/adi/pallas_call | solution.py:466
  27.3 0.8 %store.1 = (f32[384,128]{1,0:T(8,128)}, f32[384,128]{1,0:T(8,128)}) custom-call(f32[384,128]{1,0:T(8,128)S(1)} %get-tuple-element.6.half, f32[384,128]{1,0:T(8,128)S(1)} %get-tuple-element.7.adv), custom_call_target="tpu_custom_call" | custom-call | tf_op jit(solution)/shard_map/store/pallas_call | solution.py:479

commit v4 on v3

--- a/solution.py
+++ b/solution.py
@@ -6,9 +6,9 @@
 from jax.sharding import PartitionSpec as P
 
 MESH = pl.DeviceIdType.MESH
-PLACES = (6, 7, 0, 1)
-SOLVERS = tuple(8 * side + p for side in range(2) for p in PLACES)
 F32 = jnp.float32
+ORDER = (0, 4, 3, 7, 1, 5, 2, 6)
+BACK = (0, 8, 1, 9, 2, 10, 3, 11, 7, 15, 6, 14, 5, 13, 4, 12)
 
 
 class Network:
@@ -81,7 +81,7 @@
 
 def kernel(
     vel_hbm, visc_hbm, half, adv,
-    vel, visc, load, xmsg, xin, xret, xback, cmsg, cin, ymsg, yin, yret, yback, send, recv, near, far, wide, go,
+    vel, visc, load, xmsg, xin, xret, xback, cmsg, cin, ymsg, yin, yret, yback, send, recv, near, far, go,
 ):
     gx, gy = lax.axis_index("gx"), lax.axis_index("gy")
     barrier = pltpu.get_barrier_semaphore()
@@ -101,10 +101,6 @@
             tell(barrier, "gy", peer)
         for k in (12, 4, 13, 11, 5, 3, 14, 10, 6, 2, 9, 7, 8, 1, 15):
             tell(barrier, "gx", lax.rem(gx + k, 16))
-
-    @pl.when(core == 0)
-    def report():
-        tell(barrier, "gx", gx + 1)
 
     loads = [
         pltpu.make_async_copy(visc_hbm, visc, load.at[0]),
@@ -124,8 +120,13 @@
         ).start()
 
     spot = lax.rem(gy, 8)
-    solves = (spot == PLACES[0]) | (spot == PLACES[1]) | (spot == PLACES[2]) | (spot == PLACES[3])
-    rank = (gy // 8) * 4 + sum(i * (spot == p).astype(jnp.int32) for i, p in enumerate(PLACES))
+    swap = (chip == 0).astype(jnp.int32)
+    upper_first, upper_second = swap, 1 - swap
+    own_rows = (spot // 4 == upper_second).astype(jnp.int32)
+    rank = (gy // 8) * 4 + lax.rem(spot, 4)
+
+    def solver(at, upper):
+        return (at // 4) * 8 + at % 4 + 4 * upper
 
     def stay(source, start, target, to, rows):
         target[pl.ds(pl.multiple_of(to, 8), rows), :] = source[
@@ -133,24 +134,38 @@
         ]
 
     def hand_in(index, source, target, rows):
-        for at in (0, 4, 3, 7, 1, 5, 2, 6):
-
-            @pl.when(gy != SOLVERS[at])
-            def lend_row(at=at):
-                push(index, source, 16 * at, target, gy * 16, rows, gy=SOLVERS[at])
-
-        @pl.when(solves)
-        def keep_row():
-            stay(source, rank * 16, target, gy * 16, rows)
+        @pl.when(core == 0)
+        def lend_rows():
+            for at in ORDER:
+                push(index, source, 16 * at, target, gy * 16, rows, gx=gx + 1, gy=solver(at, upper_first))
+
+        @pl.when(core == 1)
+        def give_rows():
+            for at in ORDER:
+
+                @pl.when(gy != solver(at, upper_second))
+                def give_row(at=at):
+                    push(index, source, 16 * at, target, gy * 16, rows, gx=gx, gy=solver(at, upper_second))
+
+            @pl.when(own_rows == 1)
+            def keep_row():
+                stay(source, rank * 16, target, gy * 16, rows)
 
     def hand_back(index, source, target, rows):
-        for at in (0, 8, 1, 9, 2, 10, 3, 11, 7, 15, 6, 14, 5, 13, 4, 12):
-
-            @pl.when(gy != at)
-            def return_row(at=at):
-                push(index, source, 16 * at, target, rank * 16, rows, gy=at)
-
-        stay(source, gy * 16, target, rank * 16, rows)
+        @pl.when(own_rows == 0)
+        def return_rows():
+            for at in BACK:
+                push(index, source, 16 * at, target, rank * 16, rows, gx=gx - 1, gy=at)
+
+        @pl.when(own_rows == 1)
+        def pass_rows():
+            for at in BACK:
+
+                @pl.when(gy != at)
+                def pass_row(at=at):
+                    push(index, source, 16 * at, target, rank * 16, rows, gx=gx, gy=at)
+
+            stay(source, gy * 16, target, rank * 16, rows)
 
     def by_row(ref, name, rows, value=None):
         if value is None:
@@ -192,7 +207,7 @@
     for j, value in enumerate(out):
         xmsg[pl.ds(j, 8, stride=32), :] = value
 
-    pl.semaphore_wait(barrier, 8 + 5 * core)
+    pl.semaphore_wait(barrier, 8 + 4 * core)
     for k in (4, 3, 5, 2, 6, 1, 7):
         peer = lax.rem(chip + k, 8)
         push(0, xmsg, peer * 32, xin, gx * 32, 26, gx=peer * 2 + 1)
@@ -203,8 +218,8 @@
 
     @pl.when(core == 1)
     def keep():
-        for peer in around:
-            tell(near, "gy", peer)
+        tell(near, "gy", place(0, 1))
+        tell(near, "gy", place(0, -1))
         xin[pl.ds(pl.multiple_of(gx * 32, 8), 26), :] = xmsg[
             pl.ds(pl.multiple_of(chip * 32, 8), 26), :
         ]
@@ -226,7 +241,7 @@
 
     @pl.when(core == 1)
     def solve_ring():
-        pl.semaphore_wait(near, 5)
+        pl.semaphore_wait(near, 2)
         tell(far, "gy", place(0, 2))
         tell(far, "gy", place(0, -2))
 
@@ -313,9 +328,6 @@
             pl.ds(pl.multiple_of(gx * 16, 8), 12), :
         ]
         pl.semaphore_wait(far, 2)
-        tell(wide, "gy", place(0, 1))
-        tell(wide, "gy", place(0, -1))
-        pl.semaphore_wait(wide, 2)
         tell(go, "gx", gx - 1)
 
     @pl.when(core == 0)
@@ -396,17 +408,26 @@
                 inverse_a * end_a + to_b * f + to_q * lower(f, 1)
             )
 
-    @pl.when(solves)
+    def arrived_or(index, target, rows, count):
+        @pl.when(own_rows == 1)
+        def but_own():
+            arrived(index, target, (count - 1) * rows)
+
+        @pl.when(own_rows == 0)
+        def with_all():
+            arrived(index, target, count * rows)
+
+    @pl.when(core == 1)
     def solve_rows():
-        arrived(1, cin, 15 * 10)
+        arrived_or(1, cin, 10, 16)
         factors = [factor(r) for r in range(2)]
-        arrived(3, yin, 15 * 12)
+        arrived_or(3, yin, 12, 16)
         for r in range(2):
             solve_row(r, factors[r])
         hand_back(4, yret, yback, 12)
-        arrived(4, yback, 7 * 12)
-
-    @pl.when(jnp.logical_not(solves))
+        arrived_or(4, yback, 12, 8)
+
+    @pl.when(core == 0)
     def await_rows():
         arrived(4, yback, 8 * 12)
 
@@ -426,22 +447,22 @@
     departed(1, cmsg, 7 * 10)
     departed(3, ymsg, 7 * 12)
 
-    @pl.when(solves)
-    def answered():
-        departed(4, yret, 15 * 12)
-
-    @pl.when(jnp.logical_not(solves))
-    def asked():
-        departed(1, cmsg, 10)
-        departed(3, ymsg, 12)
-
     @pl.when(core == 0)
     def lent():
         departed(0, xmsg, 26)
+        departed(1, cmsg, 10)
+        departed(3, ymsg, 12)
 
     @pl.when(core == 1)
     def returned():
         departed(2, xret, 15 * 12)
+        departed(4, yret, 15 * 12)
+
+        @pl.when(own_rows == 0)
+        def all_returned():
+            departed(1, cmsg, 10)
+            departed(3, ymsg, 12)
+            departed(4, yret, 12)
 
 
 def store(half, adv, half_hbm, adv_hbm, done):
@@ -471,7 +492,7 @@
         out_specs=[vmem, vmem],
         scratch_shapes=[pltpu.VMEM((384, 128), F32), small, pltpu.SemaphoreType.DMA((2,)), large, huge, large, small, small, large, small, large, large, small]
         + [pltpu.SemaphoreType.DMA((5,)), pltpu.SemaphoreType.DMA((5,))]
-        + [pltpu.SemaphoreType.REGULAR] * 4,
+        + [pltpu.SemaphoreType.REGULAR] * 3,
         compiler_params=pltpu.CompilerParams(
             collective_id=0, has_side_effects=True, vmem_limit_bytes=32 * 1024 * 1024
         ),

time: 28.4 us -> 27.9 us (0.982)
  Pallas kernels: 27.5 us -> 27.1 us
    pallas_call x1, Pallas kernels: 26.7 us -> 26.4 us  [on_device(): pl.pallas_call(kernel, name='adi', out_shape=[jax.ShapeDtypeStruct((384,...]
where the time goes in v4:
time: 27.9 us; the launch traced here: 27.8 us
  Pallas kernels  27.1 us (97%)
  between operations  0.64 us (2%)
    pallas_call x1, Pallas kernels, on_device(): pl.pallas_call(kernel, name='adi', out_shape=[jax.ShapeDtypeStruct((384,...  26.4 us
    pallas_call x1, Pallas kernels, on_device(): pl.pallas_call(store, name='store', out_shape=[jax.ShapeDtypeStruct((384,...  0.76 us

profile of v4, /device:TPU:1, one launch (start us, length us, event | category | flops | bytes accessed | tf_op | source)
XLA Modules:
  0.0 27.8 jit_solution(10259168755675654525)
XLA Ops:
  0.6 26.4 %adi.1 = (f32[384,128]{1,0:T(8,128)S(1)}, f32[384,128]{1,0:T(8,128)S(1)}) custom-call(f32[384,128]{1,0:T(8,128)} %bitcast.4, f32[128,128]{1,0:T(8,128)} %bitcast.5), custom_call_target="tpu_custom_call" | custom-call | tf_op jit(solution)/shard_map/adi/pallas_call | solution.py:487
  27.0 0.8 %store.1 = (f32[384,128]{1,0:T(8,128)}, f32[384,128]{1,0:T(8,128)}) custom-call(f32[384,128]{1,0:T(8,128)S(1)} %get-tuple-element.6.half, f32[384,128]{1,0:T(8,128)S(1)} %get-tuple-element.7.adv), custom_call_target="tpu_custom_call" | custom-call | tf_op jit(solution)/shard_map/store/pallas_call | solution.py:500

commit v5 on v4

--- a/solution.py
+++ b/solution.py
@@ -208,6 +208,12 @@
         xmsg[pl.ds(j, 8, stride=32), :] = value
 
     pl.semaphore_wait(barrier, 8 + 4 * core)
+
+    @pl.when(core == 1)
+    def pass_on():
+        tell(near, "gy", place(0, 1))
+        tell(near, "gy", place(0, -1))
+
     for k in (4, 3, 5, 2, 6, 1, 7):
         peer = lax.rem(chip + k, 8)
         push(0, xmsg, peer * 32, xin, gx * 32, 26, gx=peer * 2 + 1)
@@ -218,8 +224,6 @@
 
     @pl.when(core == 1)
     def keep():
-        tell(near, "gy", place(0, 1))
-        tell(near, "gy", place(0, -1))
         xin[pl.ds(pl.multiple_of(gx * 32, 8), 26), :] = xmsg[
             pl.ds(pl.multiple_of(chip * 32, 8), 26), :
         ]
@@ -321,7 +325,7 @@
         out = [value[n][c] for n in names for c in range(3)]
         for j, line in enumerate(out):
             xret[pl.ds(j, 16, stride=16), :] = line
-        for k in (8, 7, 9, 5, 11, 4, 12, 3, 13, 6, 10, 2, 14, 1, 15):
+        for k in (11, 3, 13, 5, 9, 7, 15, 12, 4, 8, 10, 14, 6, 2, 1):
             peer = lax.rem(gx + k, 16)
             push(2, xret, peer * 16, xback, chip * 16, 12, gx=peer)
         xback[pl.ds(pl.multiple_of(chip * 16, 8), 12), :] = xret[

time: 27.9 us -> 27.7 us (level)
  no operation moved by 1% of the time
where the time goes in v5:
time: 27.7 us; the launch traced here: 27.6 us
  Pallas kernels  27 us (97%)
  between operations  0.64 us (2%)
    pallas_call x1, Pallas kernels, on_device(): pl.pallas_call(kernel, name='adi', out_shape=[jax.ShapeDtypeStruct((384,...  26.2 us
    pallas_call x1, Pallas kernels, on_device(): pl.pallas_call(store, name='store', out_shape=[jax.ShapeDtypeStruct((384,...  0.76 us

profile of v5, /device:TPU:1, one launch (start us, length us, event | category | flops | bytes accessed | tf_op | source)
XLA Modules:
  0.0 27.6 jit_solution(1232758155923469091)
XLA Ops:
  0.6 26.2 %adi.1 = (f32[384,128]{1,0:T(8,128)S(1)}, f32[384,128]{1,0:T(8,128)S(1)}) custom-call(f32[384,128]{1,0:T(8,128)} %bitcast.4, f32[128,128]{1,0:T(8,128)} %bitcast.5), custom_call_target="tpu_custom_call" | custom-call | tf_op jit(solution)/shard_map/adi/pallas_call | solution.py:491
  26.9 0.8 %store.1 = (f32[384,128]{1,0:T(8,128)}, f32[384,128]{1,0:T(8,128)}) custom-call(f32[384,128]{1,0:T(8,128)S(1)} %get-tuple-element.6.half, f32[384,128]{1,0:T(8,128)S(1)} %get-tuple-element.7.adv), custom_call_target="tpu_custom_call" | custom-call | tf_op jit(solution)/shard_map/store/pallas_call | solution.py:504

commit v6 on v5

--- a/solution.py
+++ b/solution.py
@@ -250,36 +250,41 @@
         tell(far, "gy", place(0, -2))
 
         arrived(0, xin, 15 * 26)
-        got = [xin[pl.ds(j, 16, stride=32), :] for j in range(26)]
-        ring = Network()
-        names = ("a", "b", "c", "d")
-        for e, (i, j) in enumerate(((0, 1), (0, 2), (0, 3), (1, 2), (1, 3), (2, 3))):
-            ring.join(names[i], names[j], got[e])
-        for i in range(4):
-            ring.add_ground(names[i], got[6 + i])
-        rhs = {names[i]: got[14 + 3 * i : 17 + 3 * i] for i in range(4)}
-        nu0, nu1, nu14, nu15 = got[10:14]
+        names = (("a", "b", "c", "d"), ("e", "f", "g", "h"))
+        ring, rhs, nu = Network(), {}, []
+        for odd in range(2):
+            name = names[odd]
+            got = [xin[pl.ds(32 * odd + j, 8, stride=64), :] for j in range(26)]
+            for e, (i, j) in enumerate(((0, 1), (0, 2), (0, 3), (1, 2), (1, 3), (2, 3))):
+                ring.join(name[i], name[j], got[e])
+            for i in range(4):
+                ring.add_ground(name[i], got[6 + i])
+                rhs[name[i]] = got[14 + 3 * i : 17 + 3 * i]
+            nu.append(got[10:14])
 
         def after(x, h):
-            return pltpu.roll(x, 16 - h, 0)
+            return pltpu.roll(x, 8 - h, 0)
 
         def before(x, h):
             return pltpu.roll(x, h, 0)
 
-        last14, last15 = before(nu14, 1), before(nu15, 1)
-        ring.join("a", "q", (last15 + nu0) * 0.5)
-        ring.join("a", "p", (last14 + nu0) * 0.125)
-        ring.join("b", "q", (last15 + nu1) * 0.125)
-        rsteps = [ring.eliminate("a")]
-        rown = [forward(rsteps[0], rhs)]
-        rsteps.append(ring.eliminate("b"))
-        rown.append(forward(rsteps[1], rhs))
-        behind = [[ring.edge[("c", "p")], ring.edge[("c", "q")]], [ring.edge[("d", "p")], ring.edge[("d", "q")]]]
+        def bridge(left, right, c, d, a, b):
+            ring.join(d, a, (left[3] + right[0]) * 0.5)
+            ring.join(c, a, (left[2] + right[0]) * 0.125)
+            ring.join(d, b, (left[3] + right[1]) * 0.125)
+
+        bridge(nu[0], nu[1], "c", "d", "e", "f")
+        bridge([before(x, 1) for x in nu[1]], nu[0], "p", "q", "a", "b")
+        rsteps, rown = [], []
+        for k in "afbecd":
+            rsteps.append(ring.eliminate(k))
+            rown.append(forward(rsteps[-1], rhs))
+        behind = [[ring.edge[("g", "p")], ring.edge[("g", "q")]], [ring.edge[("h", "p")], ring.edge[("h", "q")]]]
         onward = [[after(behind[j][i], 1) for j in range(2)] for i in range(2)]
-        ground = [ring.ground["c"] + after(ring.ground["p"], 1), ring.ground["d"] + after(ring.ground["q"], 1)]
-        inner = ring.edge[("c", "d")] + after(ring.edge[("p", "q")], 1)
+        ground = [ring.ground["g"] + after(ring.ground["p"], 1), ring.ground["h"] + after(ring.ground["q"], 1)]
+        inner = ring.edge[("g", "h")] + after(ring.edge[("p", "q")], 1)
         field = [
-            [rhs[n][c] + after(rhs[m][c], 1) for c in range(3)] for n, m in (("c", "p"), ("d", "q"))
+            [rhs[n][c] + after(rhs[m][c], 1) for c in range(3)] for n, m in (("g", "p"), ("h", "q"))
         ]
 
         def block_inverse(rest, link):
@@ -290,7 +295,7 @@
         def times(m, v):
             return [[m[i][0] * v[0][j] + m[i][1] * v[1][j] for j in range(len(v[0]))] for i in range(2)]
 
-        for h in (1, 2, 4):
+        for h in (1, 2):
             rest = [
                 ground[i] + ((behind[i][0] + behind[i][1]) + (onward[i][0] + onward[i][1]))
                 for i in range(2)
@@ -312,19 +317,20 @@
         rest = [ground[i] + (across[i][0] + across[i][1]) for i in range(2)]
         inv = block_inverse(rest, inner)
         solved = times(inv, [[ground[i]] + field[i] + [across[i][1]] for i in range(2)])
-        other = times(across, [[after(x, 8) for x in line] for line in solved])
+        other = times(across, [[after(x, 4) for x in line] for line in solved])
         ground = [ground[i] + other[i][0] for i in range(2)]
         field = [[field[i][c] + other[i][1 + c] for c in range(3)] for i in range(2)]
         inner = inner + other[0][4]
-        value_c, value_d = times(block_inverse(ground, inner), field)
-        value = {"c": value_c, "d": value_d}
-        value["p"] = [before(x, 1) for x in value_c]
-        value["q"] = [before(x, 1) for x in value_d]
+        value_g, value_h = times(block_inverse(ground, inner), field)
+        value = {"g": value_g, "h": value_h}
+        value["p"] = [before(x, 1) for x in value_g]
+        value["q"] = [before(x, 1) for x in value_h]
         for (k, unused, ratio), y in zip(rsteps[::-1], rown[::-1]):
             value[k] = [summed([y[c]] + [r * value[a][c] for a, r in ratio.items()]) for c in range(3)]
-        out = [value[n][c] for n in names for c in range(3)]
-        for j, line in enumerate(out):
-            xret[pl.ds(j, 16, stride=16), :] = line
+        for odd in range(2):
+            for i, name in enumerate(names[odd]):
+                for c in range(3):
+                    xret[pl.ds(16 * odd + 3 * i + c, 8, stride=32), :] = value[name][c]
         for k in (11, 3, 13, 5, 9, 7, 15, 12, 4, 8, 10, 14, 6, 2, 1):
             peer = lax.rem(gx + k, 16)
             push(2, xret, peer * 16, xback, chip * 16, 12, gx=peer)

time: 27.7 us -> 27.6 us (level)
  no operation moved by 1% of the time
where the time goes in v6:
time: 27.6 us; the launch traced here: 27.5 us
  Pallas kernels  26.9 us (97%)
  between operations  0.64 us (2%)
    pallas_call x1, Pallas kernels, on_device(): pl.pallas_call(kernel, name='adi', out_shape=[jax.ShapeDtypeStruct((384,...  26.1 us
    pallas_call x1, Pallas kernels, on_device(): pl.pallas_call(store, name='store', out_shape=[jax.ShapeDtypeStruct((384,...  0.76 us

profile of v6, /device:TPU:1, one launch (start us, length us, event | category | flops | bytes accessed | tf_op | source)
XLA Modules:
  0.0 27.5 jit_solution(2343843943295560758)
XLA Ops:
  0.6 26.1 %adi.1 = (f32[384,128]{1,0:T(8,128)S(1)}, f32[384,128]{1,0:T(8,128)S(1)}) custom-call(f32[384,128]{1,0:T(8,128)} %bitcast.4, f32[128,128]{1,0:T(8,128)} %bitcast.5), custom_call_target="tpu_custom_call" | custom-call | tf_op jit(solution)/shard_map/adi/pallas_call | solution.py:497
  26.7 0.8 %store.1 = (f32[384,128]{1,0:T(8,128)}, f32[384,128]{1,0:T(8,128)}) custom-call(f32[384,128]{1,0:T(8,128)S(1)} %get-tuple-element.6.half, f32[384,128]{1,0:T(8,128)S(1)} %get-tuple-element.7.adv), custom_call_target="tpu_custom_call" | custom-call | tf_op jit(solution)/shard_map/store/pallas_call | solution.py:510
